TPU v7x, 32 devices: a whole 2x2x4 slice. The times are simulated.
32 devices in a mesh: batch: 4 (over x, core), ctx: 4 (over z), head: 2 (over y).
Axes of the slice: x: 2, y: 2, z: 4, core: 2. Of those that a mesh axis runs over, the one named last changes fastest.
Arguments:
- queries: bfloat16 [2, 2048, 1536], P(None, ('batch', 'ctx'), 'head'), parts along dimension 1, may hold values from -6 to 6
- keyvals: bfloat16 [4, 2048, 1536], P(None, ('batch', 'ctx'), 'head'), parts along dimension 1, may hold values from -6 to 6
- w_out: bfloat16 [1536, 3072], P('head'), may hold values from -2.390625 to 2.390625
Outputs:
- output: bfloat16 [2048, 3072], P(('batch', 'ctx'), 'head'), parts along dimension 0
- output_tangent: bfloat16 [2048, 3072], P(('batch', 'ctx'), 'head'), parts along dimension 0
There are 4 independent parts, one for each index of `batch`. A program takes and returns all parts, laid end to end along the dimension named above; an argument that names none is the same for every part. Nothing has to cross between parts.
All inputs are finite; a program needn't handle non-finite values.
Results may differ from a plain program's by a relative error of at most 0.01.
Values may be sent and summed in bfloat16 or wider, within the bound.
A program may use at most 64 MiB of HBM per device.

v0:
```python
import functools
import math

import jax
import jax.numpy as jnp
from jax import lax
from jax.experimental import pallas as pl
from jax.experimental.pallas import tpu as pltpu
from jax.sharding import PartitionSpec as P

HD = 128
RADIUS = 2
AHEAD = 3
MESH = pl.DeviceIdType.MESH


def kernel(
    sizes, queries, keyvals, w_out, out, out_tan,
    q, kv, w, att, acc,
    q_sem, own_sem, w_sem, kv_send, kv_recv, att_send, att_recv,
    wy_send, wy_recv, wb_send, wb_recv,
):
    n_ctx, n_head, n_batch = sizes
    rows = queries.shape[1]
    width = queries.shape[2]
    heads = width // HD
    cols = out.shape[1]
    slots = min(n_ctx, 2 * RADIUS + 1)
    me = lax.axis_index("ctx")
    mine = lax.axis_index("head")
    b = lax.axis_index("batch")
    bits = [2, 1] if n_batch % 4 == 0 else [1] if n_batch % 2 == 0 else []
    pair = 2 if heads % 2 == 0 else 1
    chunk = pair * HD
    chunks = heads // pair
    piece = chunk // (1 << len(bits))

    def slot_of(tile, at):
        return tile if n_ctx <= 2 * RADIUS + 1 else tile - at + RADIUS

    def tile_rows(slot):
        return pl.ds(pl.multiple_of(slot * rows, rows), rows)

    def head_cols(h):
        return pl.ds(h * HD, HD)

    def w_rows(group, first, count):
        return pl.ds(pl.multiple_of(group * width + first, piece), count)

    def w_cols(group):
        return pl.ds(pl.multiple_of(group * cols, 128), cols)

    def sign(d):
        return 1 if d == 0 else -1

    def kv_copy(d, r, h):
        tile = me - sign(d) * (r - 1)
        to = me + sign(d)
        if r == 1:
            src = keyvals.at[:, :, head_cols(h)]
        else:
            src = kv.at[h, :, tile_rows(slot_of(tile, me)), :]
        return pltpu.make_async_remote_copy(
            src_ref=src,
            dst_ref=kv.at[h, :, tile_rows(slot_of(tile, to)), :],
            send_sem=kv_send.at[d, r - 1, h],
            recv_sem=kv_recv.at[d, r - 1, h],
            device_id={"ctx": to},
            device_id_type=MESH,
        )

    def kv_arrival(d, r, h):
        here = kv.at[h, :, tile_rows(slot_of(me - sign(d) * r, me)), :]
        return pltpu.make_async_remote_copy(
            src_ref=here, dst_ref=here,
            send_sem=kv_send.at[d, r - 1, h],
            recv_sem=kv_recv.at[d, r - 1, h],
            device_id={"ctx": me - sign(d)},
            device_id_type=MESH,
        )

    def sends(d, r):
        if d == 0:
            return (me - (r - 1) >= 0) & (me + 1 < n_ctx)
        return (me + (r - 1) < n_ctx) & (me - 1 >= 0)

    def gets(d, r):
        return me - r >= 0 if d == 0 else me + r < n_ctx

    def kv_start(r, h):
        for d in range(2):
            @pl.when(sends(d, r))
            def _():
                kv_copy(d, r, h).start()

    def kv_wait(r, h):
        for d in range(2):
            @pl.when(gets(d, r))
            def _():
                kv_arrival(d, r, h).wait_recv()

    def bit_of(bit):
        return lax.rem(b // bit, 2)

    def partner(bit):
        return b + bit - 2 * bit * bit_of(bit)

    number = 0
    for place, bit in enumerate(bits):
        number = number + bit_of(bit) * (1 << place)

    def wy_copy(d, c):
        peer = lax.rem(mine + d, n_head)
        return pltpu.make_async_remote_copy(
            src_ref=w_out.at[
                pl.ds(pl.multiple_of(c * chunk + number * piece, piece), piece), w_cols(peer)
            ],
            dst_ref=w.at[w_rows(mine, c * chunk + number * piece, piece), :],
            send_sem=wy_send.at[d - 1, c],
            recv_sem=wy_recv.at[d - 1, c],
            device_id={"head": peer},
            device_id_type=MESH,
        )

    def wy_arrival(d, c):
        sender = lax.rem(mine + n_head - d, n_head)
        here = w.at[w_rows(sender, c * chunk + number * piece, piece), :]
        return pltpu.make_async_remote_copy(
            src_ref=here, dst_ref=here,
            send_sem=wy_send.at[d - 1, c], recv_sem=wy_recv.at[d - 1, c],
            device_id={"head": sender}, device_id_type=MESH,
        )

    def wb_copy(level, d, c, receive=False):
        sender = lax.rem(mine + n_head - d, n_head)
        block = piece << level
        index = number // (1 << level)
        if receive:
            index = index + 1 - 2 * lax.rem(index, 2)
        here = w.at[w_rows(sender, c * chunk + index * block, block), :]
        return pltpu.make_async_remote_copy(
            src_ref=here, dst_ref=here,
            send_sem=wb_send.at[level, d - 1, c], recv_sem=wb_recv.at[level, d - 1, c],
            device_id={"batch": partner(bits[level])}, device_id_type=MESH,
        )

    def w_step(stage, c):
        for d in range(1, n_head):
            if stage == 0:
                wy_arrival(d, c).wait_recv()
            else:
                wb_copy(stage - 1, d, c, receive=True).wait_recv()
            if stage < len(bits):
                wb_copy(stage, d, c).start()

    def att_copy(d, h):
        return pltpu.make_async_remote_copy(
            src_ref=att.at[mine, h], dst_ref=att.at[mine, h],
            send_sem=att_send.at[d - 1, h], recv_sem=att_recv.at[d - 1, h],
            device_id={"head": lax.rem(mine + d, n_head)}, device_id_type=MESH,
        )

    def att_arrival(d, h):
        sender = lax.rem(mine + n_head - d, n_head)
        return pltpu.make_async_remote_copy(
            src_ref=att.at[sender, h], dst_ref=att.at[sender, h],
            send_sem=att_send.at[d - 1, h], recv_sem=att_recv.at[d - 1, h],
            device_id={"head": sender}, device_id_type=MESH,
        )

    def q_load():
        return pltpu.make_async_copy(queries, q, q_sem)

    def own_load(h):
        return pltpu.make_async_copy(
            keyvals.at[:, :, head_cols(h)],
            kv.at[h, :, tile_rows(slot_of(me, me)), :],
            own_sem.at[h],
        )

    def w_load():
        return pltpu.make_async_copy(
            w_out.at[:, w_cols(mine)], w.at[w_rows(mine, 0, width), :], w_sem
        )

    barrier = pltpu.get_barrier_semaphore()
    for d in range(2):
        @pl.when(sends(d, 1))
        def _():
            pl.semaphore_signal(
                barrier, inc=1, device_id={"ctx": me + sign(d)}, device_id_type=MESH
            )
    for d in range(1, n_head):
        pl.semaphore_signal(
            barrier, inc=1, device_id={"head": lax.rem(mine + d, n_head)}, device_id_type=MESH
        )
    for bit in bits:
        pl.semaphore_signal(
            barrier, inc=1, device_id={"batch": partner(bit)}, device_id_type=MESH
        )
    q_load().start()
    for h in range(heads):
        own_load(h).start()
    w_load().start()
    base = slot_of(0, me)
    for slot in range(slots):
        tile = slot - base
        @pl.when((tile < 0) | (tile >= n_ctx) | (tile - me > RADIUS) | (me - tile > RADIUS))
        def _():
            kv[:, :, slot * rows:(slot + 1) * rows, :] = jnp.zeros(
                (heads, 4, rows, HD), jnp.bfloat16
            )
    near = jnp.where(me > 0, 1, 0) + jnp.where(me + 1 < n_ctx, 1, 0)
    pl.semaphore_wait(barrier, near + (n_head - 1 + len(bits)))

    for h in range(min(AHEAD, heads)):
        kv_start(1, h)
    for d in range(1, n_head):
        for c in range(chunks):
            wy_copy(d, c).start()

    column_tile = lax.broadcasted_iota(jnp.int32, (1, slots * rows), 1) // rows - base
    visible = (
        (column_tile >= 0) & (column_tile < n_ctx)
        & (column_tile - me <= RADIUS) & (me - column_tile <= RADIUS)
    )
    scale = 1.0 / math.sqrt(HD)

    def attend(h):
        at = slice(h * HD, (h + 1) * HD)
        q_now, q_tan = q[0, :, at], q[1, :, at]
        lhs = jnp.concatenate(
            [
                jnp.concatenate([q_now, jnp.zeros_like(q_now)], axis=1),
                jnp.concatenate([q_tan, q_now], axis=1),
            ],
            axis=0,
        )
        keys = jnp.concatenate([kv[h, 0], kv[h, 2]], axis=1)
        values = jnp.concatenate([kv[h, 1], kv[h, 3]], axis=1)
        both = lax.dot_general(
            lhs, keys, (((1,), (1,)), ((), ())), preferred_element_type=jnp.float32
        )
        scores = jnp.where(visible, both[:rows], -jnp.inf)
        row_max = jnp.max(scores, axis=-1, keepdims=True)
        expo = jnp.exp2((scores - row_max) * (scale * math.log2(math.e)))
        prob = expo * (1.0 / jnp.sum(expo, axis=-1, keepdims=True))
        weighted = prob * (both[rows:] * scale)
        shift = jnp.sum(weighted, axis=-1, keepdims=True)
        left = jnp.concatenate([prob.astype(jnp.bfloat16), weighted.astype(jnp.bfloat16)], axis=0)
        mixed = jnp.dot(left, values, preferred_element_type=jnp.float32)
        attended = mixed[:rows, :HD]
        tangent = mixed[rows:, :HD] + mixed[:rows, HD:] - shift * attended
        att[mine, h, :rows] = attended.astype(jnp.bfloat16)
        att[mine, h, rows:] = tangent.astype(jnp.bfloat16)
        for d in range(1, n_head):
            att_copy(d, h).start()

    def project(group, first, count, fresh=False):
        left = jnp.concatenate([att[group, first + i] for i in range(count)], axis=1)
        part = jnp.dot(
            left, w[w_rows(group, first * HD, count * HD), :], preferred_element_type=jnp.float32
        )
        if fresh:
            acc[...] = part
        else:
            acc[...] += part

    def near_step(h):
        kv_wait(1, h)
        kv_start(2, h)
        if h + AHEAD < heads:
            kv_start(1, h + AHEAD)

    def project_far(c):
        for d in range(1, n_head):
            for i in range(pair):
                att_arrival(d, c * pair + i).wait_recv()
            project(lax.rem(mine + n_head - d, n_head), c * pair, pair)

    arrived = 0
    projected = 0

    def w_steps(step):
        done = 0
        for stage in range(len(bits) + 1):
            if 0 <= step - stage < chunks:
                w_step(stage, step - stage)
                done += stage == len(bits)
        return done

    q_load().wait()
    near_step(0)
    for h in range(heads):
        if h + 1 < heads:
            near_step(h + 1)
        own_load(h).wait()
        kv_wait(2, h)
        attend(h)
        arrived += w_steps(h)
        if h == 0:
            w_load().wait()
        if (h + 1) % pair == 0:
            project(mine, h + 1 - pair, pair, fresh=h + 1 == pair)
        elif projected < arrived and (projected + 1) * pair <= h:
            project_far(projected)
            projected += 1
    for step in range(heads, chunks + len(bits)):
        arrived += w_steps(step)
    for c in range(projected, chunks):
        project_far(c)
    out[...] = acc[:rows].astype(out.dtype)
    out_tan[...] = acc[rows:].astype(out_tan.dtype)

    for h in range(heads):
        for r in range(1, RADIUS + 1):
            for d in range(2):
                @pl.when(sends(d, r))
                def _():
                    kv_copy(d, r, h).wait_send()
        for d in range(1, n_head):
            att_copy(d, h).wait_send()
    for d in range(1, n_head):
        for c in range(chunks):
            wy_copy(d, c).wait_send()
            for level in range(len(bits)):
                wb_copy(level, d, c).wait_send()


def per_device(sizes, queries, keyvals, w_out):
    n_ctx, n_head, n_batch = sizes
    rows, width = queries.shape[1], queries.shape[2]
    heads = width // HD
    cols = w_out.shape[1] // n_head
    slots = min(n_ctx, 2 * RADIUS + 1)
    dma = pltpu.SemaphoreType.DMA
    peers = max(n_head - 1, 1)
    return pl.pallas_call(
        functools.partial(kernel, sizes),
        out_shape=[jax.ShapeDtypeStruct((rows, cols), jnp.bfloat16)] * 2,
        in_specs=[pl.BlockSpec(memory_space=pl.ANY)] * 3,
        out_specs=[pl.BlockSpec(memory_space=pltpu.VMEM)] * 2,
        scratch_shapes=[
            pltpu.VMEM((2, rows, width), jnp.bfloat16),
            pltpu.VMEM((heads, 4, slots * rows, HD), jnp.bfloat16),
            pltpu.VMEM((n_head * width, cols), jnp.bfloat16),
            pltpu.VMEM((n_head, heads, 2 * rows, HD), jnp.bfloat16),
            pltpu.VMEM((2 * rows, cols), jnp.float32),
            dma, dma((heads,)), dma,
            dma((2, RADIUS, heads)), dma((2, RADIUS, heads)),
            dma((peers, heads)), dma((peers, heads)),
            dma((peers, heads)), dma((peers, heads)),
            dma((2, peers, heads)), dma((2, peers, heads)),
        ],
        compiler_params=pltpu.CompilerParams(
            collective_id=0, has_side_effects=True, vmem_limit_bytes=63 * 1024 * 1024
        ),
        cost_estimate=pl.CostEstimate(
            flops=2 * 2 * rows * n_head * width * cols,
            bytes_accessed=16 * rows * width + 2 * w_out.size,
            transcendentals=heads * rows * slots * rows,
        ),
    )(queries, keyvals, w_out)


def solution(mesh):
    sizes = (mesh.shape["ctx"], mesh.shape["head"], mesh.shape["batch"])
    in_specs = (
        P(None, ("batch", "ctx"), "head"),
        P(None, ("batch", "ctx"), "head"),
        P("head", None),
    )
    out_specs = (P(("batch", "ctx"), "head"), P(("batch", "ctx"), "head"))
    return jax.shard_map(
        functools.partial(per_device, sizes),
        mesh=mesh, in_specs=in_specs, out_specs=out_specs, check_vma=False,
    )
```

profile of v0, /device:TPU:0, one launch (start us, length us, event | category | flops | bytes accessed | tf_op | source)
XLA Modules:
  0.0 50.9 jit_solution(8668932787816239156)
XLA Ops:
  0.6 46.7 %shard_map.50 = (bf16[128,1536]{1,0:T(8,128)(2,1)}, bf16[128,1536]{1,0:T(8,128)(2,1)}) custom-call(bf16[2,128,768]{2,1,0:T(8,128)(2,1)} %queries.1, bf16[4,128,768]{2,1,0:T(8,128)(2,1)} %keyvals.1, bf16[768,3072]{1,0:T(8,128)(2,1)} %w_out.1), custom_call_target="tpu_custom_call" | custom-call | flops 1207959552 | bytes 6291456 | tf_op jit(solution)/shard_map/pallas_call | solution.py:338
  47.4 1.8 %copy.7 = bf16[128,1536]{1,0:T(8,128)(2,1)} copy(bf16[128,1536]{1,0:T(8,128)(2,1)} %get-tuple-element.4) | data formatting | bytes 786432
  49.1 1.8 %copy.8 = bf16[128,1536]{1,0:T(8,128)(2,1)} copy(bf16[128,1536]{1,0:T(8,128)(2,1)} %get-tuple-element.5) | data formatting | bytes 786432
where the time goes:
time: 51.1 us; the launch traced here: 50.9 us
  Pallas kernels  46.7 us (91%)
  local copies, waits for them, and re-layouts  3.53 us (7%)
  between operations  0.64 us (1%)
    pallas_call x1, Pallas kernels, per_device(): pl.pallas_call(functools.partial(kernel, sizes), out_shape=[jax.ShapeDtyp...  46.7 us
    unnamed x2, local copies, waits for them, and re-layouts  3.53 us

commit v1 on v0

--- a/solution.py
+++ b/solution.py
@@ -11,6 +11,7 @@
 HD = 128
 RADIUS = 2
 AHEAD = 3
+PIECES = 4
 MESH = pl.DeviceIdType.MESH
 
 
@@ -56,12 +57,8 @@
     def kv_copy(d, r, h):
         tile = me - sign(d) * (r - 1)
         to = me + sign(d)
-        if r == 1:
-            src = keyvals.at[:, :, head_cols(h)]
-        else:
-            src = kv.at[h, :, tile_rows(slot_of(tile, me)), :]
-        return pltpu.make_async_remote_copy(
-            src_ref=src,
+        return pltpu.make_async_remote_copy(
+            src_ref=kv.at[h, :, tile_rows(slot_of(tile, me)), :],
             dst_ref=kv.at[h, :, tile_rows(slot_of(tile, to)), :],
             send_sem=kv_send.at[d, r - 1, h],
             recv_sem=kv_recv.at[d, r - 1, h],
@@ -148,6 +145,8 @@
         for d in range(1, n_head):
             if stage == 0:
                 wy_arrival(d, c).wait_recv()
+                if c + 1 < chunks:
+                    wy_copy(d, c + 1).start()
             else:
                 wb_copy(stage - 1, d, c, receive=True).wait_recv()
             if stage < len(bits):
@@ -214,10 +213,10 @@
     pl.semaphore_wait(barrier, near + (n_head - 1 + len(bits)))
 
     for h in range(min(AHEAD, heads)):
+        own_load(h).wait()
         kv_start(1, h)
     for d in range(1, n_head):
-        for c in range(chunks):
-            wy_copy(d, c).start()
+        wy_copy(d, 0).start()
 
     column_tile = lax.broadcasted_iota(jnp.int32, (1, slots * rows), 1) // rows - base
     visible = (
@@ -270,6 +269,7 @@
         kv_wait(1, h)
         kv_start(2, h)
         if h + AHEAD < heads:
+            own_load(h + AHEAD).wait()
             kv_start(1, h + AHEAD)
 
     def project_far(c):
@@ -294,7 +294,6 @@
     for h in range(heads):
         if h + 1 < heads:
             near_step(h + 1)
-        own_load(h).wait()
         kv_wait(2, h)
         attend(h)
         arrived += w_steps(h)
@@ -327,6 +326,19 @@
                 wb_copy(level, d, c).wait_send()
 
 
+def place(results, results_tan, out, out_tan, sem):
+    rows = out.shape[0] // PIECES
+    copies = [
+        pltpu.make_async_copy(src.at[pl.ds(i * rows, rows)], dst.at[pl.ds(i * rows, rows)], sem.at[n, i])
+        for n, (src, dst) in enumerate(((results, out), (results_tan, out_tan)))
+        for i in range(PIECES)
+    ]
+    for copy in copies:
+        copy.start()
+    for copy in copies:
+        copy.wait()
+
+
 def per_device(sizes, queries, keyvals, w_out):
     n_ctx, n_head, n_batch = sizes
     rows, width = queries.shape[1], queries.shape[2]
@@ -335,7 +347,7 @@
     slots = min(n_ctx, 2 * RADIUS + 1)
     dma = pltpu.SemaphoreType.DMA
     peers = max(n_head - 1, 1)
-    return pl.pallas_call(
+    results = pl.pallas_call(
         functools.partial(kernel, sizes),
         out_shape=[jax.ShapeDtypeStruct((rows, cols), jnp.bfloat16)] * 2,
         in_specs=[pl.BlockSpec(memory_space=pl.ANY)] * 3,
@@ -361,6 +373,13 @@
             transcendentals=heads * rows * slots * rows,
         ),
     )(queries, keyvals, w_out)
+    return pl.pallas_call(
+        place,
+        out_shape=[jax.ShapeDtypeStruct((rows, cols), jnp.bfloat16)] * 2,
+        in_specs=[pl.BlockSpec(memory_space=pl.ANY)] * 2,
+        out_specs=[pl.BlockSpec(memory_space=pl.ANY)] * 2,
+        scratch_shapes=[dma((2, PIECES))],
+    )(*results)
 
 
 def solution(mesh):

time: 51.1 us -> 72.3 us (1.41)
  Pallas kernels: 46.7 us -> 71.5 us
  local copies, waits for them, and re-layouts: 3.53 us -> 0 us
    pallas_call x0 -> x1, Pallas kernels: none -> 25 us  [per_device(): pl.pallas_call(place, out_shape=[jax.ShapeDtypeStruct((rows, cols), jnp.b...]
    unnamed x2 -> x0, local copies, waits for them, and re-layouts: 3.53 us -> none
where the time goes in v1:
time: 72.3 us; the launch traced here: 72.1 us
  Pallas kernels  71.5 us (99%)
    pallas_call x1, Pallas kernels, per_device(): pl.pallas_call(functools.partial(kernel, sizes), out_shape=[jax.ShapeDtyp...  46.5 us
    pallas_call x1, Pallas kernels, per_device(): pl.pallas_call(place, out_shape=[jax.ShapeDtypeStruct((rows, cols), jnp.b...  25 us

profile of v1, /device:TPU:0, one launch (start us, length us, event | category | flops | bytes accessed | tf_op | source)
XLA Modules:
  0.0 72.1 jit_solution(9550734973395091477)
XLA Ops:
  0.6 46.5 %shard_map.50 = (bf16[128,1536]{1,0:T(8,128)(2,1)}, bf16[128,1536]{1,0:T(8,128)(2,1)}) custom-call(bf16[2,128,768]{2,1,0:T(8,128)(2,1)} %queries.1, bf16[4,128,768]{2,1,0:T(8,128)(2,1)} %keyvals.1, bf16[768,3072]{1,0:T(8,128)(2,1)} %w_out.1), custom_call_target="tpu_custom_call" | custom-call | flops 1207959552 | bytes 6291456 | tf_op jit(solution)/shard_map/pallas_call | solution.py:350
  47.1 25.0 %shard_map.51 = (bf16[128,1536]{1,0:T(8,128)(2,1)}, bf16[128,1536]{1,0:T(8,128)(2,1)}) custom-call(bf16[128,1536]{1,0:T(8,128)(2,1)} %get-tuple-element.4.results, bf16[128,1536]{1,0:T(8,128)(2,1)} %get-tuple-element.5.results_tan), custom_call_target="tpu_custom_call" | custom-call | tf_op jit(solution)/shard_map/pallas_call | solution.py:376

commit v2 on v1

--- a/solution.py
+++ b/solution.py
@@ -11,6 +11,7 @@
 HD = 128
 RADIUS = 2
 AHEAD = 3
+LOOK = 2
 PIECES = 4
 MESH = pl.DeviceIdType.MESH
 
@@ -290,10 +291,11 @@
         return done
 
     q_load().wait()
-    near_step(0)
+    for h in range(min(LOOK, heads)):
+        near_step(h)
     for h in range(heads):
-        if h + 1 < heads:
-            near_step(h + 1)
+        if h + LOOK < heads:
+            near_step(h + LOOK)
         kv_wait(2, h)
         attend(h)
         arrived += w_steps(h)
@@ -326,17 +328,21 @@
                 wb_copy(level, d, c).wait_send()
 
 
-def place(results, results_tan, out, out_tan, sem):
+def place(results, results_tan, out, out_tan, held, in_sem, out_sem):
     rows = out.shape[0] // PIECES
-    copies = [
-        pltpu.make_async_copy(src.at[pl.ds(i * rows, rows)], dst.at[pl.ds(i * rows, rows)], sem.at[n, i])
-        for n, (src, dst) in enumerate(((results, out), (results_tan, out_tan)))
-        for i in range(PIECES)
-    ]
-    for copy in copies:
-        copy.start()
-    for copy in copies:
-        copy.wait()
+    loads, stores = [], []
+    for i in range(PIECES):
+        at = pl.ds(i * rows, rows)
+        for n, (src, dst) in enumerate(((results, out), (results_tan, out_tan))):
+            loads.append(pltpu.make_async_copy(src.at[at], held.at[n, at], in_sem.at[n, i]))
+            stores.append(pltpu.make_async_copy(held.at[n, at], dst.at[at], out_sem.at[n, i]))
+    for load in loads:
+        load.start()
+    for load, store in zip(loads, stores):
+        load.wait()
+        store.start()
+    for store in stores:
+        store.wait()
 
 
 def per_device(sizes, queries, keyvals, w_out):
@@ -378,7 +384,10 @@
         out_shape=[jax.ShapeDtypeStruct((rows, cols), jnp.bfloat16)] * 2,
         in_specs=[pl.BlockSpec(memory_space=pl.ANY)] * 2,
         out_specs=[pl.BlockSpec(memory_space=pl.ANY)] * 2,
-        scratch_shapes=[dma((2, PIECES))],
+        scratch_shapes=[
+            pltpu.VMEM((2, rows, cols), jnp.bfloat16), dma((2, PIECES)), dma((2, PIECES)),
+        ],
+        compiler_params=pltpu.CompilerParams(vmem_limit_bytes=63 * 1024 * 1024),
     )(*results)
 
 

time: 72.3 us -> 48.2 us (0.67)
  Pallas kernels: 71.5 us -> 47.4 us
    pallas_call x1, Pallas kernels: 25 us -> 1.99 us  [per_device(): pl.pallas_call(place, out_shape=[jax.ShapeDtypeStruct((rows, cols), jnp.b...]
    pallas_call x1, Pallas kernels: 46.5 us -> 45.4 us  [per_device(): pl.pallas_call(functools.partial(kernel, sizes), out_shape=[jax.ShapeDtyp...]
where the time goes in v2:
time: 48.2 us; the launch traced here: 48.1 us
  Pallas kernels  47.4 us (98%)
  between operations  0.64 us (1%)
    pallas_call x1, Pallas kernels, per_device(): pl.pallas_call(functools.partial(kernel, sizes), out_shape=[jax.ShapeDtyp...  45.4 us
    pallas_call x1, Pallas kernels, per_device(): pl.pallas_call(place, out_shape=[jax.ShapeDtypeStruct((rows, cols), jnp.b...  1.99 us

profile of v2, /device:TPU:0, one launch (start us, length us, event | category | flops | bytes accessed | tf_op | source)
XLA Modules:
  0.0 48.1 jit_solution(14237480345385409102)
XLA Ops:
  0.6 45.4 %shard_map.50 = (bf16[128,1536]{1,0:T(8,128)(2,1)}, bf16[128,1536]{1,0:T(8,128)(2,1)}) custom-call(bf16[2,128,768]{2,1,0:T(8,128)(2,1)} %queries.1, bf16[4,128,768]{2,1,0:T(8,128)(2,1)} %keyvals.1, bf16[768,3072]{1,0:T(8,128)(2,1)} %w_out.1), custom_call_target="tpu_custom_call" | custom-call | flops 1207959552 | bytes 6291456 | tf_op jit(solution)/shard_map/pallas_call | solution.py:356
  46.1 2.0 %shard_map.51 = (bf16[128,1536]{1,0:T(8,128)(2,1)}, bf16[128,1536]{1,0:T(8,128)(2,1)}) custom-call(bf16[128,1536]{1,0:T(8,128)(2,1)} %get-tuple-element.4.results, bf16[128,1536]{1,0:T(8,128)(2,1)} %get-tuple-element.5.results_tan), custom_call_target="tpu_custom_call" | custom-call | tf_op jit(solution)/shard_map/pallas_call | solution.py:382

commit v3 on v2

--- a/solution.py
+++ b/solution.py
@@ -18,8 +18,8 @@
 
 def kernel(
     sizes, queries, keyvals, w_out, out, out_tan,
-    q, kv, w, att, acc,
-    q_sem, own_sem, w_sem, kv_send, kv_recv, att_send, att_recv,
+    q, kv, w, att, acc, rounded,
+    q_sem, own_sem, out_sem, w_sem, kv_send, kv_recv, att_send, att_recv,
     wy_send, wy_recv, wb_send, wb_recv,
 ):
     n_ctx, n_head, n_batch = sizes
@@ -55,24 +55,24 @@
     def sign(d):
         return 1 if d == 0 else -1
 
-    def kv_copy(d, r, h):
+    def kv_copy(d, r, h, p):
         tile = me - sign(d) * (r - 1)
         to = me + sign(d)
         return pltpu.make_async_remote_copy(
-            src_ref=kv.at[h, :, tile_rows(slot_of(tile, me)), :],
-            dst_ref=kv.at[h, :, tile_rows(slot_of(tile, to)), :],
-            send_sem=kv_send.at[d, r - 1, h],
-            recv_sem=kv_recv.at[d, r - 1, h],
+            src_ref=kv.at[h, pl.ds(2 * p, 2), tile_rows(slot_of(tile, me)), :],
+            dst_ref=kv.at[h, pl.ds(2 * p, 2), tile_rows(slot_of(tile, to)), :],
+            send_sem=kv_send.at[d, r - 1, h, p],
+            recv_sem=kv_recv.at[d, r - 1, h, p],
             device_id={"ctx": to},
             device_id_type=MESH,
         )
 
-    def kv_arrival(d, r, h):
-        here = kv.at[h, :, tile_rows(slot_of(me - sign(d) * r, me)), :]
+    def kv_arrival(d, r, h, p):
+        here = kv.at[h, pl.ds(2 * p, 2), tile_rows(slot_of(me - sign(d) * r, me)), :]
         return pltpu.make_async_remote_copy(
             src_ref=here, dst_ref=here,
-            send_sem=kv_send.at[d, r - 1, h],
-            recv_sem=kv_recv.at[d, r - 1, h],
+            send_sem=kv_send.at[d, r - 1, h, p],
+            recv_sem=kv_recv.at[d, r - 1, h, p],
             device_id={"ctx": me - sign(d)},
             device_id_type=MESH,
         )
@@ -85,17 +85,17 @@
     def gets(d, r):
         return me - r >= 0 if d == 0 else me + r < n_ctx
 
-    def kv_start(r, h):
+    def kv_start(r, h, p):
         for d in range(2):
             @pl.when(sends(d, r))
             def _():
-                kv_copy(d, r, h).start()
-
-    def kv_wait(r, h):
+                kv_copy(d, r, h, p).start()
+
+    def kv_wait(r, h, p):
         for d in range(2):
             @pl.when(gets(d, r))
             def _():
-                kv_arrival(d, r, h).wait_recv()
+                kv_arrival(d, r, h, p).wait_recv()
 
     def bit_of(bit):
         return lax.rem(b // bit, 2)
@@ -171,12 +171,21 @@
     def q_load():
         return pltpu.make_async_copy(queries, q, q_sem)
 
-    def own_load(h):
-        return pltpu.make_async_copy(
-            keyvals.at[:, :, head_cols(h)],
-            kv.at[h, :, tile_rows(slot_of(me, me)), :],
-            own_sem.at[h],
-        )
+    def own_load(h, p):
+        return [
+            pltpu.make_async_copy(
+                keyvals.at[2 * i + p, :, head_cols(h)],
+                kv.at[h, 2 * p + i, tile_rows(slot_of(me, me)), :],
+                own_sem.at[h, 2 * p + i],
+            )
+            for i in range(2)
+        ]
+
+    def own_send(h):
+        for p in range(2):
+            for load in own_load(h, p):
+                load.wait()
+            kv_start(1, h, p)
 
     def w_load():
         return pltpu.make_async_copy(
@@ -200,7 +209,9 @@
         )
     q_load().start()
     for h in range(heads):
-        own_load(h).start()
+        for p in range(2):
+            for load in own_load(h, p):
+                load.start()
     w_load().start()
     base = slot_of(0, me)
     for slot in range(slots):
@@ -214,8 +225,7 @@
     pl.semaphore_wait(barrier, near + (n_head - 1 + len(bits)))
 
     for h in range(min(AHEAD, heads)):
-        own_load(h).wait()
-        kv_start(1, h)
+        own_send(h)
     for d in range(1, n_head):
         wy_copy(d, 0).start()
 
@@ -236,8 +246,8 @@
             ],
             axis=0,
         )
-        keys = jnp.concatenate([kv[h, 0], kv[h, 2]], axis=1)
-        values = jnp.concatenate([kv[h, 1], kv[h, 3]], axis=1)
+        kv_wait(2, h, 0)
+        keys = jnp.concatenate([kv[h, 0], kv[h, 1]], axis=1)
         both = lax.dot_general(
             lhs, keys, (((1,), (1,)), ((), ())), preferred_element_type=jnp.float32
         )
@@ -248,6 +258,8 @@
         weighted = prob * (both[rows:] * scale)
         shift = jnp.sum(weighted, axis=-1, keepdims=True)
         left = jnp.concatenate([prob.astype(jnp.bfloat16), weighted.astype(jnp.bfloat16)], axis=0)
+        kv_wait(2, h, 1)
+        values = jnp.concatenate([kv[h, 2], kv[h, 3]], axis=1)
         mixed = jnp.dot(left, values, preferred_element_type=jnp.float32)
         attended = mixed[:rows, :HD]
         tangent = mixed[rows:, :HD] + mixed[:rows, HD:] - shift * attended
@@ -256,6 +268,27 @@
         for d in range(1, n_head):
             att_copy(d, h).start()
 
+    block = 512 if cols % 512 == 0 else cols
+
+    def out_copies(i):
+        at = pl.ds(i * block, block)
+        return [
+            pltpu.make_async_copy(rounded.at[pl.ds(n * rows, rows), at], to.at[:, at], out_sem.at[n, i])
+            for n, to in enumerate((out, out_tan))
+        ]
+
+    def finish(group, first, count):
+        left = jnp.concatenate([att[group, first + i] for i in range(count)], axis=1)
+        for i in range(cols // block):
+            at = slice(i * block, (i + 1) * block)
+            part = jnp.dot(
+                left, w[w_rows(group, first * HD, count * HD), at],
+                preferred_element_type=jnp.float32,
+            )
+            rounded[:, at] = (acc[:, at] + part).astype(rounded.dtype)
+            for copy in out_copies(i):
+                copy.start()
+
     def project(group, first, count, fresh=False):
         left = jnp.concatenate([att[group, first + i] for i in range(count)], axis=1)
         part = jnp.dot(
@@ -267,17 +300,18 @@
             acc[...] += part
 
     def near_step(h):
-        kv_wait(1, h)
-        kv_start(2, h)
+        for p in range(2):
+            kv_wait(1, h, p)
+            kv_start(2, h, p)
         if h + AHEAD < heads:
-            own_load(h + AHEAD).wait()
-            kv_start(1, h + AHEAD)
+            own_send(h + AHEAD)
 
     def project_far(c):
         for d in range(1, n_head):
             for i in range(pair):
                 att_arrival(d, c * pair + i).wait_recv()
-            project(lax.rem(mine + n_head - d, n_head), c * pair, pair)
+            last = c == chunks - 1 and d == n_head - 1
+            (finish if last else project)(lax.rem(mine + n_head - d, n_head), c * pair, pair)
 
     arrived = 0
     projected = 0
@@ -296,7 +330,6 @@
     for h in range(heads):
         if h + LOOK < heads:
             near_step(h + LOOK)
-        kv_wait(2, h)
         attend(h)
         arrived += w_steps(h)
         if h == 0:
@@ -310,15 +343,13 @@
         arrived += w_steps(step)
     for c in range(projected, chunks):
         project_far(c)
-    out[...] = acc[:rows].astype(out.dtype)
-    out_tan[...] = acc[rows:].astype(out_tan.dtype)
-
     for h in range(heads):
         for r in range(1, RADIUS + 1):
             for d in range(2):
                 @pl.when(sends(d, r))
                 def _():
-                    kv_copy(d, r, h).wait_send()
+                    kv_copy(d, r, h, 0).wait_send()
+                    kv_copy(d, r, h, 1).wait_send()
         for d in range(1, n_head):
             att_copy(d, h).wait_send()
     for d in range(1, n_head):
@@ -326,6 +357,9 @@
             wy_copy(d, c).wait_send()
             for level in range(len(bits)):
                 wb_copy(level, d, c).wait_send()
+    for i in range(cols // block):
+        for copy in out_copies(i):
+            copy.wait()
 
 
 def place(results, results_tan, out, out_tan, held, in_sem, out_sem):
@@ -357,15 +391,16 @@
         functools.partial(kernel, sizes),
         out_shape=[jax.ShapeDtypeStruct((rows, cols), jnp.bfloat16)] * 2,
         in_specs=[pl.BlockSpec(memory_space=pl.ANY)] * 3,
-        out_specs=[pl.BlockSpec(memory_space=pltpu.VMEM)] * 2,
+        out_specs=[pl.BlockSpec(memory_space=pl.ANY)] * 2,
         scratch_shapes=[
             pltpu.VMEM((2, rows, width), jnp.bfloat16),
             pltpu.VMEM((heads, 4, slots * rows, HD), jnp.bfloat16),
             pltpu.VMEM((n_head * width, cols), jnp.bfloat16),
             pltpu.VMEM((n_head, heads, 2 * rows, HD), jnp.bfloat16),
             pltpu.VMEM((2 * rows, cols), jnp.float32),
-            dma, dma((heads,)), dma,
-            dma((2, RADIUS, heads)), dma((2, RADIUS, heads)),
+            pltpu.VMEM((2 * rows, cols), jnp.bfloat16),
+            dma, dma((heads, 4)), dma((2, cols // HD)), dma,
+            dma((2, RADIUS, heads, 2)), dma((2, RADIUS, heads, 2)),
             dma((peers, heads)), dma((peers, heads)),
             dma((peers, heads)), dma((peers, heads)),
             dma((2, peers, heads)), dma((2, peers, heads)),

time: 48.2 us -> 48.6 us (level)
  no operation moved by 1% of the time
where the time goes in v3:
time: 48.6 us; the launch traced here: 48.4 us
  Pallas kernels  47.8 us (98%)
  between operations  0.64 us (1%)
    pallas_call x1, Pallas kernels, per_device(): pl.pallas_call(functools.partial(kernel, sizes), out_shape=[jax.ShapeDtyp...  45.8 us
    pallas_call x1, Pallas kernels, per_device(): pl.pallas_call(place, out_shape=[jax.ShapeDtypeStruct((rows, cols), jnp.b...  1.99 us

profile of v3, /device:TPU:0, one launch (start us, length us, event | category | flops | bytes accessed | tf_op | source)
XLA Modules:
  0.0 48.4 jit_solution(15579127590751875259)
XLA Ops:
  0.6 45.8 %shard_map.50 = (bf16[128,1536]{1,0:T(8,128)(2,1)}, bf16[128,1536]{1,0:T(8,128)(2,1)}) custom-call(bf16[2,128,768]{2,1,0:T(8,128)(2,1)} %queries.1, bf16[4,128,768]{2,1,0:T(8,128)(2,1)} %keyvals.1, bf16[768,3072]{1,0:T(8,128)(2,1)} %w_out.1), custom_call_target="tpu_custom_call" | custom-call | flops 1207959552 | bytes 6291456 | tf_op jit(solution)/shard_map/pallas_call | solution.py:390
  46.4 2.0 %shard_map.51 = (bf16[128,1536]{1,0:T(8,128)(2,1)}, bf16[128,1536]{1,0:T(8,128)(2,1)}) custom-call(bf16[128,1536]{1,0:T(8,128)(2,1)} %get-tuple-element.4.results, bf16[128,1536]{1,0:T(8,128)(2,1)} %get-tuple-element.5.results_tan), custom_call_target="tpu_custom_call" | custom-call | tf_op jit(solution)/shard_map/pallas_call | solution.py:417
